TPU v7x, 1024 devices: a whole 4x4x32 slice. The times are simulated.
1024 devices in a mesh: row: 16 (over x, z_hi, core), col: 64 (over z_lo, y).
Axes of the slice: x: 4, y: 4, z: 32 (z_hi: 2, z_lo: 16; z = z_hi * 16 + z_lo), core: 2. Of those that a mesh axis runs over, the one named last changes fastest.
Arguments:
- x_blocks: bfloat16 [3072, 128, 128], P(('row', 'col')), may hold values from -2 to 2
- x_cols: int32 [3072], P(('row', 'col')), may hold values from 0 to 8191, as said below
- q_blocks: bfloat16 [64, 48, 128, 128], P('col', 'row'), may hold values from -2 to 2
- q_cols: int32 [64, 48], P('col', 'row'), may hold values from 0 to 8191, as said below
Outputs:
- symmetric: float32 [64, 64, 128, 128], P('col', None, 'row')
Inputs may be any that keep to these rules, and one draw needn't show every extreme that they name: For some c0 shared by x_cols and q_cols, the 48 block columns of window row i (in either array) are distinct and lie among the 128 columns (c0 + i + t) mod 8192, t = 0 ... 127. `q_cols`: as for x_cols, with the same c0.
All inputs are finite; a program needn't handle non-finite values.
Results may differ from a plain program's by a relative error of at most 0.00035.
Values may be sent and summed in bfloat16 or wider, within the bound.
A program may use at most 64 MiB of HBM per device.

v0:
```python
import jax
import jax.numpy as jnp
from jax import lax
from jax.sharding import PartitionSpec as P

NNZ = 48


def shards(x_blocks, x_cols, q_blocks, q_cols):
    n_row = lax.axis_size("row")
    n_col = lax.axis_size("col")
    width = x_blocks.shape[-1]
    slab = width // n_row
    own_rows = x_blocks.shape[0] * n_col // NNZ
    own_cols = q_blocks.shape[0]
    q_panel, q_index = (
        lax.all_gather(q_blocks, "row", axis=1, tiled=True),
        lax.all_gather(q_cols, "row", axis=1, tiled=True),
    )
    x_panel, x_index = (
        lax.all_gather(x_blocks, "col", axis=0, tiled=True),
        lax.all_gather(x_cols, "col", axis=0, tiled=True),
    )
    x_rows = x_panel.reshape(own_rows, NNZ, width, width)
    x_where = x_index.reshape(own_rows, NNZ)
    match = (x_where[:, :, None, None] == q_index[None, None, :, :]).astype(jnp.bfloat16)
    aligned = jnp.einsum("ipjq,jqyz->ijpyz", match, q_panel, preferred_element_type=jnp.bfloat16)
    tile = jnp.einsum("ipxz,ijpyz->ijxy", x_rows, aligned, preferred_element_type=jnp.float32)
    direct = tile.reshape(own_rows, own_cols, n_row, slab, width)
    flipped = jnp.swapaxes(tile, 2, 3).reshape(own_rows, own_cols, n_row, slab, width)
    stacked = jnp.stack([direct, flipped])
    moved = lax.all_to_all(stacked, "row", split_axis=3, concat_axis=1, tiled=True)
    first_half = lax.all_to_all(moved[0][:, :, 0], "col", split_axis=0, concat_axis=1, tiled=True)
    second_half = jnp.swapaxes(moved[1][:, :, 0], 0, 1)
    return 0.5 * (first_half + second_half)


def solution(mesh):
    placed = (
        P(("row", "col"), None, None),
        P(("row", "col")),
        P("col", "row", None, None),
        P("col", "row"),
    )
    return jax.shard_map(
        shards, mesh=mesh, in_specs=placed, out_specs=P("col", None, "row", None), check_vma=False
    )
```

profile of v0, /device:TPU:1, one launch (start us, length us, event | category | flops | bytes accessed | tf_op | source)
XLA Modules:
  0.0 960.4 jit_solution(6936487758938932471)
XLA Ops:
  6.5 0.0 all-gather.3.cloned.1.call-start
  6.5 0.7 all-gather.3.cloned.1.call-update
  7.3 0.0 all-gather.5.cloned.1.call-start
  7.3 0.7 all-gather.5.cloned.1.call-update
  8.0 1.3 dynamic-slice
  9.9 0.9 dynamic-update-slice
  10.8 37.3 %all-reduce = s32[192]{0:T(256)S(1)} all-reduce(s32[192]{0:T(256)S(1)} %dynamic-update-slice), channel_id=1, replica_groups=mesh['row'=16,'col'=64] {'col'}, use_global_device_ids=true, to_apply=%add | all-reduce | flops 192 | bytes 1536
  48.1 0.1 eq.20
  48.2 1.3 dynamic-slice.1
  50.1 0.8 bitcast_dynamic-update-slice_fusion
  50.9 32.5 %all-reduce.1 = s32[48]{0:T(128)S(1)} all-reduce(s32[48]{0:T(128)S(1)} %bitcast_dynamic-update-slice_fusion), channel_id=1, replica_groups=mesh['row'=16,'col'=64] {'row'}, use_global_device_ids=true, to_apply=%add.1 | all-reduce | flops 48 | bytes 384
  83.4 74.4 %all-gather.3.cloned.1.call-done = bf16[1,48,128,128]{3,2,0,1:T(8,128)(2,1)} async-done(((bf16[1,3,128,128]{3,2,0,1:T(8,128)(2,1)}), bf16[1,48,128,128]{3,2,0,1:T(8,128)(2,1)}) %all-gather.3.cloned.1.call-update) | async-done | bytes 1572880 | tf_op jit(solution)/shard_map/all_gather | solution.py:17
  157.8 6.0 fusion.2
  163.8 665.8 %all-gather.5.cloned.1.call-done = bf16[192,128,128]{2,1,0:T(8,128)(2,1)} async-done(((bf16[3,128,128]{2,1,0:T(8,128)(2,1)}), bf16[192,128,128]{2,1,0:T(8,128)(2,1)}) %all-gather.5.cloned.1.call-update) | async-done | bytes 6291472 | tf_op jit(solution)/shard_map/all_gather | solution.py:21
  829.6 6.4 fusion
  836.0 0.1 copy.17
  836.2 0.1 copy.18
  836.3 83.2 %all_to_all.27 = f32[2,4,1,16,8,128]{5,4,1,2,0,3:T(8,128)S(1)} all-to-all(f32[2,4,1,16,8,128]{5,4,1,2,0,3:T(8,128)S(1)} %copy.18), channel_id=1, replica_groups=mesh['row'=16,'col'=64] {'row'}, dimensions={3} | all-to-all | bytes 1048576 | tf_op jit(solution)/shard_map/all_to_all | solution.py:32
  919.6 33.2 %all_to_all.28 = f32[64,1,8,128]{3,2,1,0:T(8,128)S(1)} all-to-all(f32[64,1,8,128]{3,2,1,0:T(8,128)S(1)} %bitcast.41), channel_id=1, replica_groups=mesh['row'=16,'col'=64] {'col'}, dimensions={0} | all-to-all | bytes 524288 | tf_op jit(solution)/shard_map/all_to_all | solution.py:33
  952.8 0.7 fusion.5
  (5 shorter events, 0.1 us)
Async XLA Ops:
  6.5 151.3 %all-gather.3.cloned.1.call-start = ((), (), s32[]{:S(2)}) async-start(), calls=%async_computation.2 | async-start | bytes 1671168 | tf_op jit(solution)/shard_map/all_gather | solution.py:17
  7.3 822.4 %all-gather.5.cloned.1.call-start = ((), (), s32[]{:S(2)}) async-start(), calls=%async_computation.3 | async-start | bytes 6389760 | tf_op jit(solution)/shard_map/all_gather | solution.py:21
Sparse Core Ops, SparseCore 0:
  11.8 145.9 all-gather.2
  160.5 669.1 all-gather.4
where the time goes:
time: 965 us; the launch traced here: 960 us
  waiting for transfers between devices  742 us (77%)
  blocking collectives  186 us (19%)
  between operations  14.8 us (2%)
  matrix products  12.4 us (1%)
    all_gather x1, waiting for transfers between devices, shards(): lax.all_gather(x_blocks, 'col', axis=0, tiled=True)  666 us
    all_to_all x1, blocking collectives, shards(): lax.all_to_all(stacked, 'row', split_axis=3, concat_axis=1, tiled=True)  83.2 us
    all_gather x1, waiting for transfers between devices, shards(): lax.all_gather(q_blocks, 'row', axis=1, tiled=True)  74.4 us
    unnamed x2, blocking collectives  69.8 us
    all_to_all x1, blocking collectives, shards(): lax.all_to_all(moved[0][:, :, 0], 'col', split_axis=0, concat_axis=1, til...  33.2 us
  transfers between devices with their start and end apart: 2, of which 2 were waited for; matrix products, arithmetic and copies ran while one was open for 1% of the time, Pallas kernels for 0%

commit v1 on v0

v1 whole, which is shorter than its diff:
```python
import functools

import jax
import jax.numpy as jnp
from jax import lax
from jax.experimental import pallas as pl
from jax.experimental.pallas import tpu as pltpu
from jax.sharding import PartitionSpec as P

MESH = pl.DeviceIdType.MESH
NZ = 32
STEPS = 16
V_AT = 5
WIN = 132
GROUP = 4


def where_am_i():
    row, col = lax.axis_index("row"), lax.axis_index("col")
    x, zh, core = row // 4, (row // 2) % 2, row % 2
    zl, y = col // 4, col % 4
    return x, y, zh, zl, core


def device(x, y, z, core):
    return (x * 4 + (z // 16) * 2 + core, (z % 16) * 4 + y)


def gather_kernel(xb, qb, meta, w, wm, v, vm, wp_send, wp_recv, v1_send, v1_recv,
                  v2_send, v2_recv, ring_send, ring_recv):
    x, y, zh, zl, core = where_am_i()
    z = zh * 16 + zl
    a = zl // 4
    me = device(x, y, z, core)
    chip = x * 4 + y

    def is_me(dev):
        return (dev[0] == me[0]) & (dev[1] == me[1])

    x_plane = 4 * x + 2 * zh + core
    x_dst = [device(zl % 4, y, x_plane + 16 * h, 1) for h in range(2)]
    q_dst = [device(x, y, zl + 16 * h, 0) for h in range(2)]

    bar = pltpu.get_barrier_semaphore()

    def greet(k, carry):
        chip2 = (chip + k // 2) % 16
        core2 = (core + k % 2) % 2
        pl.semaphore_signal(bar, inc=1, device_id=device(chip2 // 4, chip2 % 4, z, core2), device_id_type=MESH)
        return carry
    lax.fori_loop(1, 32, greet, 0)
    right = device(x, y, (z + 1) % NZ, core)
    left = device(x, y, (z + NZ - 1) % NZ, core)
    for dev in (right, left, device(x, y, (z + 16) % NZ, 0), device(x, y, (z + 16) % NZ, 1)):
        pl.semaphore_signal(bar, inc=1, device_id=dev, device_id_type=MESH)
    for b in range(4):
        src = (zl, (4 * b + x) * 4 + y)

        @pl.when((core == 1) & jnp.logical_not(is_me(src)))
        def _():
            pl.semaphore_signal(bar, inc=1, device_id=src, device_id_type=MESH)
    own_pieces = sum(jnp.where(is_me(dev), 1, 0) for dev in x_dst)
    pl.semaphore_wait(bar, 37 - own_pieces)

    sent = []

    def send(src, dst, ssem, rsem, dev):
        mine = is_me(dev)
        copy = pltpu.make_async_remote_copy(src, dst, ssem, rsem, device_id=dev, device_id_type=MESH)

        @pl.when(jnp.logical_not(mine))
        def _():
            copy.start()

        @pl.when(mine)
        def _():
            pltpu.make_async_copy(src, dst, rsem).start()
        sent.append((mine, copy))

    for s in range(4):
        x_to = device((x + a) % 4, s, z, 0)
        send(xb.at[:, s], w.at[z, y * 2 + core], wp_send.at[0, s, 0], wp_recv.at[0], x_to)
        send(meta.at[0], wm.at[z, y * 2 + core], wp_send.at[0, s, 1], wp_recv.at[1], x_to)
        q_to = device((y + a) % 4, s, z, 1)
        send(qb.at[:, s], w.at[z, x * 2 + core], wp_send.at[1, s, 0], wp_recv.at[0], q_to)
        send(meta.at[1], wm.at[z, x * 2 + core], wp_send.at[1, s, 1], wp_recv.at[1], q_to)
    for h in range(2):
        slot = (zl % 4) * 4 + y
        send(xb.at[:, :, h], v.at[slot, a], v1_send.at[0, h, 0], v1_recv.at[0], x_dst[h])
        send(meta.at[0], vm.at[slot, a], v1_send.at[0, h, 1], v1_recv.at[1], x_dst[h])
        part = zh * 2 + core
        send(qb.at[:, :, h], v.at[chip, part], v1_send.at[1, h, 0], v1_recv.at[0], q_dst[h])
        send(meta.at[1], vm.at[chip, part], v1_send.at[1, h, 1], v1_recv.at[1], q_dst[h])

    w[NZ] = jnp.zeros(w.shape[1:], w.dtype)
    v[16] = jnp.zeros(v.shape[1:], v.dtype)

    def ring(way, step, part):
        plane = (z + NZ - step) % NZ if way == 0 else (z + step) % NZ
        ref = wm.at[plane] if part == 2 else w.at[plane, pl.ds(part * 4, 4)]
        return pltpu.make_async_remote_copy(
            ref, ref, ring_send.at[way, step, part], ring_recv.at[way, step, part],
            device_id=right if way == 0 else left, device_id_type=MESH)

    def arrived(way, step, part):
        plane = (z + NZ - step - 1) % NZ if way == 0 else (z + step + 1) % NZ
        ref = wm.at[plane] if part == 2 else w.at[plane, pl.ds(part * 4, 4)]
        pltpu.make_async_copy(ref, ref, ring_recv.at[way, step, part]).wait()

    pltpu.make_async_copy(w.at[z], w.at[z], wp_recv.at[0]).wait()
    pltpu.make_async_copy(wm.at[z], wm.at[z], wp_recv.at[1]).wait()
    for part in range(3):
        for way in range(2):
            ring(way, 0, part).start()

    def ring_step(step, carry):
        for part in range(3):
            for way in range(2):
                arrived(way, step - 1, part)
                ring(way, step, part).start()
        return carry
    lax.fori_loop(1, V_AT, ring_step, 0)

    pltpu.make_async_copy(v.at[chip], v.at[chip], v1_recv.at[0]).wait()
    pltpu.make_async_copy(vm.at[chip], vm.at[chip], v1_recv.at[1]).wait()

    def share(k, n):
        chip2 = (chip + k) % 16
        ref = (v, vm)[n].at[chip]
        return pltpu.make_async_remote_copy(
            ref, ref, v2_send.at[k, n], v2_recv.at[chip, n],
            device_id=device(chip2 // 4, chip2 % 4, z, core), device_id_type=MESH)

    def share_start(k, carry):
        for n in range(2):
            share(k, n).start()
        return carry
    lax.fori_loop(1, 16, share_start, 0)

    lax.fori_loop(V_AT, STEPS - 1, ring_step, 0)
    last = STEPS - 1
    for way, part in ((0, 0), (1, 1), (0, 2)):
        arrived(way, last - 1, part)
        ring(way, last, part).start()
    for way, part in ((1, 0), (0, 1), (1, 2)):
        arrived(way, last - 1, part)

    def share_end(k, carry):
        chip2 = (chip + k) % 16
        for n in range(2):
            ref = (v, vm)[n].at[chip2]
            pltpu.make_async_copy(ref, ref, v2_recv.at[chip2, n]).wait()
            share(k, n).wait_send()
        return carry
    lax.fori_loop(1, 16, share_end, 0)
    for mine, copy in sent:
        @pl.when(jnp.logical_not(mine))
        def _():
            copy.wait_send()

    def ring_sent(step, carry):
        for part in range(3):
            for way in range(2):
                ring(way, step, part).wait_send()
        return carry
    lax.fori_loop(0, last, ring_sent, 0)
    for way, part in ((0, 0), (1, 1), (0, 2)):
        arrived(way, last, part)
        ring(way, last, part).wait_send()


def gather(xb, qb, meta):
    bf, i32 = jnp.bfloat16, jnp.int32
    dma = pltpu.SemaphoreType.DMA
    vmem = pl.BlockSpec(memory_space=pltpu.VMEM)
    return pl.pallas_call(
        gather_kernel,
        out_shape=(
            jax.ShapeDtypeStruct((NZ + 1, 8, 3, 2, 16, 128), bf),
            jax.ShapeDtypeStruct((NZ, 8, 1, 128), i32),
            jax.ShapeDtypeStruct((17, 4, 3, 4, 16, 128), bf),
            jax.ShapeDtypeStruct((16, 4, 1, 128), i32),
        ),
        in_specs=[vmem] * 3,
        out_specs=(vmem,) * 4,
        scratch_shapes=[
            dma((2, 4, 2)), dma((2,)), dma((2, 2, 2)), dma((2,)),
            dma((16, 2)), dma((16, 2)), dma((2, STEPS, 3)), dma((2, STEPS, 3)),
        ],
        compiler_params=pltpu.CompilerParams(
            collective_id=0, has_side_effects=True, vmem_limit_bytes=40 * 2**20),
        name="gather",
    )(xb, qb, meta)


def tables(wm, vm):
    core = lax.axis_index("row") % 2
    w_cols = wm[:, :, 0, :3]
    v_cols = vm[:, :, 0, :3]
    w_ids = jnp.arange(NZ * 24, dtype=jnp.int32)
    v_ids = jnp.arange(192, dtype=jnp.int32)

    def rows_w(t):
        from_x = t.reshape(2, 4, 4, 4, 2, 3).transpose(1, 0, 4, 2, 3, 5).reshape(16, 48)
        from_q = t.reshape(2, 4, 4, 24).transpose(1, 2, 0, 3).reshape(16, 48)
        return jnp.where(core == 0, from_x, from_q)

    def rows_v(t):
        from_q = t.reshape(4, 4, 12).transpose(1, 0, 2).reshape(4, 48)
        from_x = t.reshape(16, 4, 3).transpose(1, 0, 2).reshape(4, 48)
        return jnp.where(core == 0, from_q, from_x)
    wc, wi = rows_w(w_cols), rows_w(w_ids)
    vc, vi = rows_v(v_cols), rows_v(v_ids)
    first = vc[0, 0]
    off = ((vc - first + 4096) & 8191) - 4096 - jnp.arange(4, dtype=jnp.int32)[:, None]
    base = first + jnp.min(off)
    places = jnp.arange(WIN, dtype=jnp.int32)

    def table(cols, ids, none):
        hit = ((cols - base) & 8191)[:, :, None] == places
        return none + jnp.sum(jnp.where(hit, ids[:, :, None] - none, 0), axis=1)
    return table(vc, vi, 192), table(wc, wi, NZ * 24)


def product_kernel(tv, tw, v, w, out):
    out[...] = jnp.zeros_like(out)

    def step(g, carry):
        vs, ws = [], []
        for u in range(GROUP):
            at = g * GROUP + u
            vs.append(jnp.concatenate([v[tv[c, at]].reshape(64, 128) for c in range(4)], axis=0))
            ws.append(jnp.concatenate([w[tw[m, at]].reshape(32, 128) for m in range(16)], axis=0))
        left = jnp.concatenate(vs, axis=1)
        right = jnp.concatenate(ws, axis=1)
        out[...] += lax.dot_general(left, right, (((1,), (1,)), ((), ())), preferred_element_type=jnp.float32)
        return carry
    lax.fori_loop(0, WIN // GROUP, step, 0)


def product(tv, tw, v, w):
    vmem = pl.BlockSpec(memory_space=pltpu.VMEM)
    smem = pl.BlockSpec(memory_space=pltpu.SMEM)
    return pl.pallas_call(
        product_kernel,
        out_shape=jax.ShapeDtypeStruct((256, 512), jnp.float32),
        in_specs=[smem, smem, vmem, vmem],
        out_specs=vmem,
        compiler_params=pltpu.CompilerParams(vmem_limit_bytes=40 * 2**20),
        name="product",
    )(tv, tw, v, w)


def exchange_kernel(t, out, got, send_sem, recv_sem):
    x, y, zh, zl, core = where_am_i()
    z = zh * 16 + zl
    chip = x * 4 + y
    mine = chip * 2 + core
    bar = pltpu.get_barrier_semaphore()

    def peer(k):
        other = (mine + k) % 32
        px, py, pc = other // 8, (other // 2) % 4, other % 2
        return other, px, py, pc

    def greet(k, carry):
        _, px, py, pc = peer(k)
        pl.semaphore_signal(bar, inc=1, device_id=device(px, py, z, pc), device_id_type=MESH)
        return carry
    lax.fori_loop(1, 32, greet, 0)
    pl.semaphore_wait(bar, 31)

    def copy(k):
        _, px, py, pc = peer(k)
        return pltpu.make_async_remote_copy(
            t.at[py, px, pc], got.at[mine], send_sem.at[k], recv_sem.at[mine],
            device_id=device(px, py, z, pc), device_id_type=MESH)

    def start(k, carry):
        copy(k).start()
        return carry
    lax.fori_loop(1, 32, start, 0)
    own = pltpu.make_async_copy(t.at[y, x, core], got.at[mine], recv_sem.at[mine])
    own.start()
    own.wait()

    def finish(k, carry):
        other, _, _, _ = peer(k)
        pltpu.make_async_copy(got.at[other], got.at[other], recv_sem.at[other]).wait()
        copy(k).wait_send()
        return carry
    lax.fori_loop(1, 32, finish, 0)

    lane = lax.broadcasted_iota(jnp.int32, (8, 128), 1) // 32
    for xs in range(4):
        halves = []
        for cs in range(2):
            rows = {}
            for m4 in range(4):
                part = [got[(xs * 4 + ys) * 2 + cs, :, m4 * 128:(m4 + 1) * 128] for ys in range(4)]
                for mid in range(4):
                    acc = None
                    for ys in range(4):
                        turn = ((ys - mid) * 32) % 128
                        piece = pltpu.roll(part[ys], turn, axis=1) if turn else part[ys]
                        acc = piece if acc is None else jnp.where(lane == ys, piece, acc)
                    if cs == 0:
                        j = 16 * ((xs - m4) % 4) + 4 * mid + m4
                    else:
                        j = 16 * m4 + 4 * mid + (xs - m4) % 4
                    rows[j] = acc
            halves.append(rows)
        for j in halves[0]:
            out[j] = 0.5 * (halves[0][j] + halves[1][j])


def exchange(t):
    dma = pltpu.SemaphoreType.DMA
    vmem = pl.BlockSpec(memory_space=pltpu.VMEM)
    return pl.pallas_call(
        exchange_kernel,
        out_shape=jax.ShapeDtypeStruct((64, 8, 128), jnp.float32),
        in_specs=[vmem],
        out_specs=vmem,
        scratch_shapes=[pltpu.VMEM((32, 8, 512), jnp.float32), dma((32,)), dma((32,))],
        compiler_params=pltpu.CompilerParams(
            collective_id=1, has_side_effects=True, vmem_limit_bytes=16 * 2**20),
        name="exchange",
    )(t)


def shards(x_blocks, x_cols, q_blocks, q_cols):
    xb = x_blocks.reshape(3, 4, 2, 16, 128)
    qb = q_blocks.reshape(3, 4, 2, 16, 128)
    meta = jnp.pad(jnp.stack([x_cols, q_cols[0]]), ((0, 0), (0, 125))).reshape(2, 1, 128)
    w, wm, v, vm = gather(xb, qb, meta)
    tv, tw = tables(wm, vm)
    t = product(tv, tw, v.reshape(17 * 12, 4, 16, 128), w.reshape((NZ + 1) * 24, 2, 16, 128))
    return exchange(t.reshape(4, 4, 2, 8, 512))[None]


def solution(mesh):
    placed = (
        P(("row", "col"), None, None),
        P(("row", "col")),
        P("col", "row", None, None),
        P("col", "row"),
    )
    return jax.shard_map(
        shards, mesh=mesh, in_specs=placed, out_specs=P("col", None, "row", None), check_vma=False
    )
```

time: 965 us -> 190 us (0.20)
  the two profiles are of different devices: /device:TPU:1 before, /device:TPU:57 now
where the time goes in v1:
time: 190 us; the launch traced here: 189 us
  Pallas kernels  161 us (85%)
  local copies, waits for them, and re-layouts  22.5 us (12%)
  other arithmetic  4.65 us (2%)
    pallas_call x1, Pallas kernels, gather(): pl.pallas_call(gather_kernel, out_shape=(jax.ShapeDtypeStruct((NZ + 1, 8,...  130 us
    pallas_call x1, Pallas kernels, exchange(): pl.pallas_call(exchange_kernel, out_shape=jax.ShapeDtypeStruct((64, 8, 12...  18.1 us
    pallas_call x1, Pallas kernels, product(): pl.pallas_call(product_kernel, out_shape=jax.ShapeDtypeStruct((256, 512),...  12.6 us
    unnamed x9, local copies, waits for them, and re-layouts  8.03 us

profile of v1, /device:TPU:57, one launch (start us, length us, event | category | flops | bytes accessed | tf_op | source)
XLA Modules:
  0.0 189.5 jit_solution(12296853807926326932)
XLA Ops:
  0.0 0.7 pad_add_fusion
  1.9 0.7 reshape.438
  2.6 0.7 reshape.471
  3.9 0.7 iota.147
  5.8 0.7 reshape.467
  6.5 0.7 reshape.445
  7.8 0.7 reshape.459
  8.5 0.7 iota.159
  9.8 0.9 copy-done.2
  10.7 0.9 copy-done.3
  11.6 130.3 %gather.1 = (bf16[33,8,3,2,16,128]{5,4,3,2,1,0:T(8,128)(2,1)S(1)}, s32[32,8,1,128]{3,2,1,0:T(1,128)S(1)}, bf16[17,4,3,4,16,128]{5,4,3,2,1,0:T(8,128)(2,1)S(1)}, s32[16,4,1,128]{3,2,1,0:T(1,128)S(1)}) custom-call(bf16[3,4,2,16,128]{4,3,2,1,0:T(8,128)(2,1)S(1)} %bitcast.37, bf16[3,4,2,16,128]{4,3,2,1,0:T(8,128)(2,1)S(1)} %bitcast.38, s32[2,1,128]{2,1,0:T(1,128)S(1)} %bitcast.39), custom_call_target="tpu_custom_call" | custom-call | tf_op jit(solution)/shard_map/gather/pallas_call | solution.py:176
  141.9 2.7 %copy-done = bf16[33,8,3,2,16,128]{5,4,3,2,1,0:T(8,128)(2,1)} copy-done((bf16[33,8,3,2,16,128]{5,4,3,2,1,0:T(8,128)(2,1)}, bf16[33,8,3,2,16,128]{5,4,3,2,1,0:T(8,128)(2,1)S(1)}, u32[]{:S(2)}) %copy-start) | copy-done | bytes 6488088
  144.7 0.7 reshape.431
  145.6 0.7 broadcast_select_fusion
  147.0 1.3 fusion.5
  149.7 0.7 select_add_fusion.1
  150.5 1.5 slice_reduce_fusion.1
  152.0 1.0 reshape.485
  153.1 0.9 copy.26
  154.2 0.8 select_add_fusion
  155.3 2.8 %copy-done.1 = bf16[33,8,3,2,16,128]{5,4,3,2,1,0:T(8,128)(2,1)S(1)} copy-done((bf16[33,8,3,2,16,128]{5,4,3,2,1,0:T(8,128)(2,1)S(1)}, bf16[33,8,3,2,16,128]{5,4,3,2,1,0:T(8,128)(2,1)}, u32[]{:S(2)}) %copy-start.1) | copy-done | bytes 6488088
  158.1 12.6 %product.1 = f32[256,512]{1,0:T(8,128)S(1)} custom-call(s32[4,132]{1,0:T(4,128)S(1)} %broadcast_add_fusion.1.tv, s32[16,132]{1,0:T(8,128)S(1)} %broadcast_add_fusion.tw, bf16[204,4,16,128]{3,2,1,0:T(8,128)(2,1)S(1)} %bitcast.34, bf16[792,2,16,128]{3,2,1,0:T(8,128)(2,1)S(1)} %bitcast.33), custom_call_target="tpu_custom_call" | custom-call | tf_op jit(solution)/shard_map/product/pallas_call | solution.py:244
  170.7 18.1 %exchange.1 = f32[64,8,128]{2,1,0:T(8,128)S(1)} custom-call(f32[4,4,2,8,512]{4,3,2,1,0:T(8,128)S(1)} %bitcast.35), custom_call_target="tpu_custom_call" | custom-call | tf_op jit(solution)/shard_map/exchange/pallas_call | solution.py:320
  188.8 0.7 copy.28
  (42 shorter events, 6.2 us)
Async XLA Ops:
  9.8 0.9 copy-start.2
  10.7 0.9 copy-start.3
  141.8 2.7 %copy-start = (bf16[33,8,3,2,16,128]{5,4,3,2,1,0:T(8,128)(2,1)}, bf16[33,8,3,2,16,128]{5,4,3,2,1,0:T(8,128)(2,1)S(1)}, u32[]{:S(2)}) copy-start(bf16[33,8,3,2,16,128]{5,4,3,2,1,0:T(8,128)(2,1)S(1)} %get-tuple-element.12) | copy-start | bytes 19464196
  155.3 2.8 %copy-start.1 = (bf16[33,8,3,2,16,128]{5,4,3,2,1,0:T(8,128)(2,1)S(1)}, bf16[33,8,3,2,16,128]{5,4,3,2,1,0:T(8,128)(2,1)}, u32[]{:S(2)}) copy-start(bf16[33,8,3,2,16,128]{5,4,3,2,1,0:T(8,128)(2,1)} %copy-done) | copy-start | bytes 19464196

commit v2 on v1

v2 whole, which is shorter than its diff:
```python
import jax
import jax.numpy as jnp
from jax import lax
from jax.experimental import pallas as pl
from jax.experimental.pallas import tpu as pltpu
from jax.sharding import PartitionSpec as P

MESH = pl.DeviceIdType.MESH
NZ = 32
STEPS = 16
PARTS = 4
WIN = 132
GROUP = 4


def where_am_i():
    row, col = lax.axis_index("row"), lax.axis_index("col")
    x, zh, core = row // 4, (row // 2) % 2, row % 2
    zl, y = col // 4, col % 4
    return x, y, zh, zl, core


def device(x, y, z, core):
    return (x * 4 + (z // 16) * 2 + core, (z % 16) * 4 + y)


def gather_kernel(xb, qb, meta, w, wm, v, vm, w_send, w_recv, v_send, v_recv, ring_send, ring_recv):
    x, y, zh, zl, core = where_am_i()
    z = zh * 16 + zl
    a = zl // 4
    me = device(x, y, z, core)
    chip = x * 4 + y
    right = device(x, y, (z + 1) % NZ, core)
    left = device(x, y, (z + NZ - 1) % NZ, core)

    def is_me(dev):
        return (dev[0] == me[0]) & (dev[1] == me[1])

    bar = pltpu.get_barrier_semaphore()

    def greet(k, carry):
        chip2 = (chip + k // 2) % 16
        core2 = (core + k % 2) % 2
        pl.semaphore_signal(bar, inc=1, device_id=device(chip2 // 4, chip2 % 4, z, core2), device_id_type=MESH)
        return carry
    lax.fori_loop(1, 32, greet, 0)
    for dev in (right, left):
        pl.semaphore_signal(bar, inc=1, device_id=dev, device_id_type=MESH)
    pl.semaphore_wait(bar, 33)

    sent = []

    def send(src, dst, ssem, rsem, dev):
        mine = is_me(dev)
        copy = pltpu.make_async_remote_copy(src, dst, ssem, rsem, device_id=dev, device_id_type=MESH)

        @pl.when(jnp.logical_not(mine))
        def _():
            copy.start()

        @pl.when(mine)
        def _():
            pltpu.make_async_copy(src, dst, rsem).start()
        sent.append((mine, copy))

    for s in range(4):
        x_to = device((x + a) % 4, s, z, 0)
        send(xb.at[:, s], w.at[z, y * 2 + core], w_send.at[0, s, 0], w_recv.at[0], x_to)
        send(meta.at[0], wm.at[z, y * 2 + core], w_send.at[0, s, 1], w_recv.at[1], x_to)
        q_to = device((y + a) % 4, s, z, 1)
        send(qb.at[:, s], w.at[z, x * 2 + core], w_send.at[1, s, 0], w_recv.at[0], q_to)
        send(meta.at[1], wm.at[z, x * 2 + core], w_send.at[1, s, 1], w_recv.at[1], q_to)

    w[NZ] = jnp.zeros(w.shape[1:], w.dtype)
    v[64] = jnp.zeros(v.shape[1:], v.dtype)

    size = 8 // PARTS

    def chunk(plane, part):
        return wm.at[plane] if part == PARTS else w.at[plane, pl.ds(part * size, size)]

    def ring(way, step, part):
        ref = chunk((z + NZ - step) % NZ if way == 0 else (z + step) % NZ, part)
        return pltpu.make_async_remote_copy(
            ref, ref, ring_send.at[way, step, part], ring_recv.at[way, step, part],
            device_id=right if way == 0 else left, device_id_type=MESH)

    def arrived(way, step, part):
        ref = chunk((z + NZ - step - 1) % NZ if way == 0 else (z + step + 1) % NZ, part)
        pltpu.make_async_copy(ref, ref, ring_recv.at[way, step, part]).wait()

    own = (x + 4 - a) % 4

    def pass_on(plane):
        half, quarter, place = plane // 16, (plane % 16) // 4, plane % 4

        @pl.when((core == 0) & (half == (zl // 2) % 2) & (quarter == own))
        def _():
            def one(k, carry):
                chip2 = (chip + k) % 16
                to = device(chip2 // 4, chip2 % 4, z, 1)
                for yy in range(4):
                    g = quarter * 16 + place * 4 + yy
                    pltpu.make_async_remote_copy(
                        w.at[plane, yy * 2 + zl % 2, :, zh], v.at[g, :, y], v_send.at[0], v_recv.at[0],
                        device_id=to, device_id_type=MESH).start()

                    @pl.when(chip2 % 4 == y)
                    def _():
                        pltpu.make_async_remote_copy(
                            wm.at[plane, yy * 2 + zl % 2], vm.at[g], v_send.at[1], v_recv.at[1],
                            device_id=to, device_id_type=MESH).start()
                return carry
            lax.fori_loop(0, 16, one, 0)

        @pl.when((core == 1) & (plane % 16 == zl))
        def _():
            def one(k, carry):
                chip2 = (chip + k) % 16
                to = device(chip2 // 4, chip2 % 4, z, 0)
                g = own * 16 + half * 8
                pltpu.make_async_remote_copy(
                    w.at[plane, :, :, zh], v.at[pl.ds(g, 8), :, y], v_send.at[0], v_recv.at[0],
                    device_id=to, device_id_type=MESH).start()

                @pl.when(chip2 % 4 == y)
                def _():
                    pltpu.make_async_remote_copy(
                        wm.at[plane], vm.at[pl.ds(g, 8)], v_send.at[1], v_recv.at[1],
                        device_id=to, device_id_type=MESH).start()
                return carry
            lax.fori_loop(0, 16, one, 0)

    pltpu.make_async_copy(w.at[z], w.at[z], w_recv.at[0]).wait()
    pltpu.make_async_copy(wm.at[z], wm.at[z], w_recv.at[1]).wait()
    for part in range(PARTS + 1):
        for way in range(2):
            ring(way, 0, part).start()
    pass_on(z)

    def ring_step(step, carry):
        for part in range(PARTS + 1):
            for way in range(2):
                arrived(way, step - 1, part)
                ring(way, step, part).start()
        pass_on((z + NZ - step) % NZ)
        pass_on((z + step) % NZ)
        return carry
    last = STEPS - 1
    lax.fori_loop(1, last, ring_step, 0)
    ends = [(0 if part < PARTS // 2 else 1, part) for part in range(PARTS + 1)]
    for way, part in ends:
        arrived(way, last - 1, part)
        ring(way, last, part).start()
    for way, part in ends:
        arrived(1 - way, last - 1, part)
    pass_on((z + NZ - last) % NZ)
    pass_on((z + last) % NZ)
    for way, part in ends:
        arrived(way, last, part)
    pass_on((z + 16) % NZ)

    for mine, copy in sent:
        @pl.when(jnp.logical_not(mine))
        def _():
            copy.wait_send()

    def ring_sent(step, carry):
        for part in range(PARTS + 1):
            for way in range(2):
                ring(way, step, part).wait_send()
        return carry
    lax.fori_loop(0, last, ring_sent, 0)
    for way, part in ends:
        ring(way, last, part).wait_send()
    rows = v.at[pl.ds(0, 64)]
    for n, ref in enumerate((rows, vm)):
        pltpu.make_async_copy(ref, ref, v_recv.at[n]).wait()
        pltpu.make_async_copy(ref, ref, v_send.at[n]).wait()


def gather(xb, qb, meta):
    bf, i32 = jnp.bfloat16, jnp.int32
    dma = pltpu.SemaphoreType.DMA
    vmem = pl.BlockSpec(memory_space=pltpu.VMEM)
    return pl.pallas_call(
        gather_kernel,
        out_shape=(
            jax.ShapeDtypeStruct((NZ + 1, 8, 3, 2, 16, 128), bf),
            jax.ShapeDtypeStruct((NZ, 8, 1, 128), i32),
            jax.ShapeDtypeStruct((65, 3, 4, 16, 128), bf),
            jax.ShapeDtypeStruct((64, 1, 128), i32),
        ),
        in_specs=[vmem] * 3,
        out_specs=(vmem,) * 4,
        scratch_shapes=[
            dma((2, 4, 2)), dma((2,)), dma((2,)), dma((2,)),
            dma((2, STEPS, PARTS + 1)), dma((2, STEPS, PARTS + 1)),
        ],
        compiler_params=pltpu.CompilerParams(
            collective_id=0, has_side_effects=True, vmem_limit_bytes=40 * 2**20),
        name="gather",
    )(xb, qb, meta)


def product_kernel(wm, vm, v_hbm, w_hbm, out, v, w, rows, tab, v_sem, w_sem, tab_sem):
    x, y, zh, zl, core = where_am_i()
    v_in = pltpu.make_async_copy(v_hbm, v, v_sem)
    w_in = pltpu.make_async_copy(w_hbm, w, w_sem)
    v_in.start()
    w_in.start()

    v_cols, w_cols = vm[...], wm[...]
    first = v_cols[0:1, 0:1]
    row = lax.broadcasted_iota(jnp.int32, (64, 128), 0) // 16
    lane = lax.broadcasted_iota(jnp.int32, (64, 128), 1)
    off = ((v_cols - first + 4096) & 8191) - 4096 - row
    off = jnp.where(lane < 3, off, 8192).astype(jnp.float32)
    least = jnp.min(jnp.min(off, axis=1, keepdims=True), axis=0, keepdims=True)
    base = first + least.astype(jnp.int32)

    def hits(cols, none):
        n = cols.shape[0]
        place = lax.broadcasted_iota(jnp.int32, (n, 256), 1)
        ids = (lax.broadcasted_iota(jnp.int32, (n, 256), 0) * 3 - none).astype(jnp.float32)
        total = jnp.zeros((n, 256), jnp.float32)
        for k in range(3):
            total += jnp.where(((cols[:, k:k + 1] - base) & 8191) == place, ids + k, 0.0)
        return total

    none_v, none_w = 192, NZ * 24
    in_v = jnp.sum(hits(v_cols, none_v).reshape(4, 16, 256), axis=1)
    in_w = hits(w_cols, none_w).reshape(2, 4, 4, 8, 256)
    from_q = jnp.sum(jnp.sum(in_w, axis=0), axis=2)
    over_place = in_w[:, :, 0] + in_w[:, :, 1] + in_w[:, :, 2] + in_w[:, :, 3]
    odd = lax.broadcasted_iota(jnp.int32, (2, 4, 8, 256), 2) % 2
    from_x = [jnp.sum(jnp.where(odd == n, over_place, 0.0), axis=2) for n in range(2)]
    for b in range(4):
        for mid in range(4):
            of_x = from_x[mid % 2][mid // 2, b:b + 1]
            of_q = from_q[(3 - b) % 4, mid:mid + 1]
            for xs in range(3):
                of_q = jnp.where(x == xs, from_q[(xs - b) % 4, mid:mid + 1], of_q)
            m = b * 4 + mid
            rows[m:m + 1] = jnp.where(core == 0, of_x, of_q).astype(jnp.int32) + none_w
    rows[16:20] = in_v.astype(jnp.int32) + none_v
    tab_in = pltpu.make_async_copy(rows, tab, tab_sem)
    tab_in.start()
    out[...] = jnp.zeros_like(out)
    tab_in.wait()
    v_in.wait()
    w_in.wait()

    def step(g, carry):
        vs, ws = [], []
        for u in range(GROUP):
            at = g * GROUP + u
            vs.append(jnp.concatenate([v[tab[16 + c, at]].reshape(64, 128) for c in range(4)], axis=0))
            ws.append(jnp.concatenate([w[tab[m, at]].reshape(32, 128) for m in range(16)], axis=0))
        left = jnp.concatenate(vs, axis=1)
        right = jnp.concatenate(ws, axis=1)
        out[...] += lax.dot_general(left, right, (((1,), (1,)), ((), ())), preferred_element_type=jnp.float32)
        return carry
    lax.fori_loop(0, WIN // GROUP, step, 0)


def product(wm, vm, v, w):
    vmem = pl.BlockSpec(memory_space=pltpu.VMEM)
    hbm = pl.BlockSpec(memory_space=pl.ANY)
    dma = pltpu.SemaphoreType.DMA
    return pl.pallas_call(
        product_kernel,
        out_shape=jax.ShapeDtypeStruct((256, 512), jnp.float32),
        in_specs=[vmem, vmem, hbm, hbm],
        out_specs=vmem,
        scratch_shapes=[
            pltpu.VMEM(v.shape, v.dtype), pltpu.VMEM(w.shape, w.dtype),
            pltpu.VMEM((24, 256), jnp.int32), pltpu.SMEM((24, 256), jnp.int32),
            dma, dma, dma,
        ],
        compiler_params=pltpu.CompilerParams(vmem_limit_bytes=40 * 2**20),
        name="product",
    )(wm, vm, v, w)


def exchange_kernel(t, out, half, total, got, half_send, half_recv, send_sem, recv_sem):
    x, y, zh, zl, core = where_am_i()
    z = zh * 16 + zl
    chip = x * 4 + y
    bar = pltpu.get_barrier_semaphore()

    def greet(k, carry):
        chip2 = (chip + k) % 16
        pl.semaphore_signal(bar, inc=1, device_id=device(chip2 // 4, chip2 % 4, z, core), device_id_type=MESH)
        return carry
    lax.fori_loop(1, 16, greet, 0)
    partner = device(x, y, z, 1 - core)
    pl.semaphore_signal(bar, inc=1, device_id=partner, device_id_type=MESH)
    pl.semaphore_wait(bar, 16)

    swap = pltpu.make_async_remote_copy(
        t.at[:, :, 1 - core], half, half_send, half_recv, device_id=partner, device_id_type=MESH)
    swap.start()
    swap.wait_recv()
    total[...] = t[:, :, core] + half[...]

    def copy(k):
        chip2 = (chip + k) % 16
        return pltpu.make_async_remote_copy(
            total.at[chip2 % 4, chip2 // 4], got.at[chip], send_sem.at[k], recv_sem.at[chip],
            device_id=device(chip2 // 4, chip2 % 4, z, core), device_id_type=MESH)

    def start(k, carry):
        copy(k).start()
        return carry
    lax.fori_loop(1, 16, start, 0)
    own = pltpu.make_async_copy(total.at[y, x], got.at[chip], recv_sem.at[chip])
    own.start()
    own.wait()
    swap.wait_send()

    def finish(k, carry):
        chip2 = (chip + k) % 16
        pltpu.make_async_copy(got.at[chip2], got.at[chip2], recv_sem.at[chip2]).wait()
        copy(k).wait_send()
        return carry
    lax.fori_loop(1, 16, finish, 0)

    lane = lax.broadcasted_iota(jnp.int32, (8, 128), 1) // 32
    for xs in range(4):
        for b in range(4):
            part = [got[xs * 4 + ys, :, b * 128:(b + 1) * 128] for ys in range(4)]
            for mid in range(4):
                acc = None
                for ys in range(4):
                    turn = ((ys - mid) * 32) % 128
                    piece = pltpu.roll(part[ys], turn, axis=1) if turn else part[ys]
                    acc = piece if acc is None else jnp.where(lane == ys, piece, acc)
                out[16 * ((xs - b) % 4) + 4 * mid + b] = 0.5 * acc


def exchange(t):
    dma = pltpu.SemaphoreType.DMA
    vmem = pl.BlockSpec(memory_space=pltpu.VMEM)
    f32 = jnp.float32
    return pl.pallas_call(
        exchange_kernel,
        out_shape=jax.ShapeDtypeStruct((64, 8, 128), f32),
        in_specs=[vmem],
        out_specs=vmem,
        scratch_shapes=[
            pltpu.VMEM((4, 4, 8, 512), f32), pltpu.VMEM((4, 4, 8, 512), f32), pltpu.VMEM((16, 8, 512), f32),
            dma, dma, dma((16,)), dma((16,)),
        ],
        compiler_params=pltpu.CompilerParams(
            collective_id=1, has_side_effects=True, vmem_limit_bytes=16 * 2**20),
        name="exchange",
    )(t)


def shards(x_blocks, x_cols, q_blocks, q_cols):
    xb = x_blocks.reshape(3, 4, 2, 16, 128)
    qb = q_blocks.reshape(3, 4, 2, 16, 128)
    meta = jnp.pad(jnp.stack([x_cols, q_cols[0]]), ((0, 0), (0, 125))).reshape(2, 1, 128)
    w, wm, v, vm = gather(xb, qb, meta)
    t = product(
        wm.reshape(NZ * 8, 128), vm.reshape(64, 128),
        v.reshape(65 * 3, 4, 16, 128), w.reshape((NZ + 1) * 24, 2, 16, 128))
    return exchange(t.reshape(4, 4, 2, 8, 512))[None]


def solution(mesh):
    placed = (
        P(("row", "col"), None, None),
        P(("row", "col")),
        P("col", "row", None, None),
        P("col", "row"),
    )
    return jax.shard_map(
        shards, mesh=mesh, in_specs=placed, out_specs=P("col", None, "row", None), check_vma=False
    )
```

time: 190 us -> 152 us (0.80)
  the two profiles are of different devices: /device:TPU:57 before, /device:TPU:1 now
where the time goes in v2:
time: 152 us
  Pallas kernels  149 us (98%)
  local copies, waits for them, and re-layouts  2.49 us (2%)
    pallas_call x1, Pallas kernels, gather(): pl.pallas_call(gather_kernel, out_shape=(jax.ShapeDtypeStruct((NZ + 1, 8,...  115 us
    pallas_call x1, Pallas kernels, exchange(): pl.pallas_call(exchange_kernel, out_shape=jax.ShapeDtypeStruct((64, 8, 12...  20 us
    pallas_call x1, Pallas kernels, product(): pl.pallas_call(product_kernel, out_shape=jax.ShapeDtypeStruct((256, 512),...  13.8 us

profile of v2, /device:TPU:1, one launch (start us, length us, event | category | flops | bytes accessed | tf_op | source)
XLA Modules:
  0.0 151.8 jit_solution(9657616562605496687)
XLA Ops:
  0.0 0.7 pad_add_fusion
  0.7 0.0 copy-start
  0.7 0.9 copy-done
  1.6 0.0 copy-start.1
  1.6 0.9 copy-done.1
  2.5 114.8 %gather.1 = (bf16[33,8,3,2,16,128]{5,4,3,2,1,0:T(8,128)(2,1)S(1)}, s32[32,8,1,128]{3,2,1,0:T(1,128)S(1)}, bf16[65,3,4,16,128]{4,3,2,1,0:T(8,128)(2,1)S(1)}, s32[64,1,128]{2,1,0:T(1,128)S(1)}) custom-call(bf16[3,4,2,16,128]{4,3,2,1,0:T(8,128)(2,1)S(1)} %bitcast.15, bf16[3,4,2,16,128]{4,3,2,1,0:T(8,128)(2,1)S(1)} %bitcast.16, s32[2,1,128]{2,1,0:T(1,128)S(1)} %bitcast.18), custom_call_target="tpu_custom_call" | custom-call | tf_op jit(solution)/shard_map/gather/pallas_call | solution.py:186
  117.3 13.8 %product.1 = f32[256,512]{1,0:T(8,128)S(1)} custom-call(s32[256,128]{1,0:T(8,128)S(1)} %bitcast.14, s32[64,128]{1,0:T(8,128)S(1)} %bitcast.17, bf16[195,4,16,128]{3,2,1,0:T(8,128)(2,1)S(1)} %bitcast.11, bf16[792,2,16,128]{3,2,1,0:T(8,128)(2,1)S(1)} %bitcast.10), custom_call_target="tpu_custom_call" | custom-call | tf_op jit(solution)/shard_map/product/pallas_call | solution.py:271
  131.2 20.0 %exchange.1 = f32[64,8,128]{2,1,0:T(8,128)S(1)} custom-call(f32[4,4,2,8,512]{4,3,2,1,0:T(8,128)S(1)} %bitcast.12), custom_call_target="tpu_custom_call" | custom-call | tf_op jit(solution)/shard_map/exchange/pallas_call | solution.py:346
  151.1 0.7 copy.6
  (1 shorter events, 0.0 us)
Async XLA Ops:
  0.7 0.9 copy-start
  1.6 0.9 copy-start.1

commit v3 on v2

--- a/solution.py
+++ b/solution.py
@@ -10,7 +10,7 @@
 STEPS = 16
 PARTS = 4
 WIN = 132
-GROUP = 4
+GROUP = 33
 
 
 def where_am_i():
@@ -65,8 +65,8 @@
 
     for s in range(4):
         x_to = device((x + a) % 4, s, z, 0)
-        send(xb.at[:, s], w.at[z, y * 2 + core], w_send.at[0, s, 0], w_recv.at[0], x_to)
-        send(meta.at[0], wm.at[z, y * 2 + core], w_send.at[0, s, 1], w_recv.at[1], x_to)
+        send(xb.at[:, s], w.at[z, core * 4 + y], w_send.at[0, s, 0], w_recv.at[0], x_to)
+        send(meta.at[0], wm.at[z, core * 4 + y], w_send.at[0, s, 1], w_recv.at[1], x_to)
         q_to = device((y + a) % 4, s, z, 1)
         send(qb.at[:, s], w.at[z, x * 2 + core], w_send.at[1, s, 0], w_recv.at[0], q_to)
         send(meta.at[1], wm.at[z, x * 2 + core], w_send.at[1, s, 1], w_recv.at[1], q_to)
@@ -99,17 +99,17 @@
             def one(k, carry):
                 chip2 = (chip + k) % 16
                 to = device(chip2 // 4, chip2 % 4, z, 1)
-                for yy in range(4):
-                    g = quarter * 16 + place * 4 + yy
+                g = quarter * 16 + place * 4
+                mine = pl.ds(zl % 2 * 4, 4)
+                pltpu.make_async_remote_copy(
+                    w.at[plane, mine, :, zh], v.at[pl.ds(g, 4), :, y], v_send.at[0], v_recv.at[0],
+                    device_id=to, device_id_type=MESH).start()
+
+                @pl.when(chip2 % 4 == y)
+                def _():
                     pltpu.make_async_remote_copy(
-                        w.at[plane, yy * 2 + zl % 2, :, zh], v.at[g, :, y], v_send.at[0], v_recv.at[0],
+                        wm.at[plane, mine], vm.at[pl.ds(g, 4)], v_send.at[1], v_recv.at[1],
                         device_id=to, device_id_type=MESH).start()
-
-                    @pl.when(chip2 % 4 == y)
-                    def _():
-                        pltpu.make_async_remote_copy(
-                            wm.at[plane, yy * 2 + zl % 2], vm.at[g], v_send.at[1], v_recv.at[1],
-                            device_id=to, device_id_type=MESH).start()
                 return carry
             lax.fori_loop(0, 16, one, 0)
 
@@ -183,6 +183,7 @@
     bf, i32 = jnp.bfloat16, jnp.int32
     dma = pltpu.SemaphoreType.DMA
     vmem = pl.BlockSpec(memory_space=pltpu.VMEM)
+    hbm = pl.BlockSpec(memory_space=pltpu.HBM)
     return pl.pallas_call(
         gather_kernel,
         out_shape=(
@@ -191,7 +192,7 @@
             jax.ShapeDtypeStruct((65, 3, 4, 16, 128), bf),
             jax.ShapeDtypeStruct((64, 1, 128), i32),
         ),
-        in_specs=[vmem] * 3,
+        in_specs=[hbm, hbm, vmem],
         out_specs=(vmem,) * 4,
         scratch_shapes=[
             dma((2, 4, 2)), dma((2,)), dma((2,)), dma((2,)),
@@ -203,12 +204,8 @@
     )(xb, qb, meta)
 
 
-def product_kernel(wm, vm, v_hbm, w_hbm, out, v, w, rows, tab, v_sem, w_sem, tab_sem):
+def product_kernel(wm, vm, v, w, out, rows, tab, tab_sem):
     x, y, zh, zl, core = where_am_i()
-    v_in = pltpu.make_async_copy(v_hbm, v, v_sem)
-    w_in = pltpu.make_async_copy(w_hbm, w, w_sem)
-    v_in.start()
-    w_in.start()
 
     v_cols, w_cols = vm[...], wm[...]
     first = v_cols[0:1, 0:1]
@@ -233,8 +230,8 @@
     in_w = hits(w_cols, none_w).reshape(2, 4, 4, 8, 256)
     from_q = jnp.sum(jnp.sum(in_w, axis=0), axis=2)
     over_place = in_w[:, :, 0] + in_w[:, :, 1] + in_w[:, :, 2] + in_w[:, :, 3]
-    odd = lax.broadcasted_iota(jnp.int32, (2, 4, 8, 256), 2) % 2
-    from_x = [jnp.sum(jnp.where(odd == n, over_place, 0.0), axis=2) for n in range(2)]
+    of_core = lax.broadcasted_iota(jnp.int32, (2, 4, 8, 256), 2) // 4
+    from_x = [jnp.sum(jnp.where(of_core == n, over_place, 0.0), axis=2) for n in range(2)]
     for b in range(4):
         for mid in range(4):
             of_x = from_x[mid % 2][mid // 2, b:b + 1]
@@ -248,8 +245,6 @@
     tab_in.start()
     out[...] = jnp.zeros_like(out)
     tab_in.wait()
-    v_in.wait()
-    w_in.wait()
 
     def step(g, carry):
         vs, ws = [], []
@@ -266,17 +261,14 @@
 
 def product(wm, vm, v, w):
     vmem = pl.BlockSpec(memory_space=pltpu.VMEM)
-    hbm = pl.BlockSpec(memory_space=pl.ANY)
-    dma = pltpu.SemaphoreType.DMA
     return pl.pallas_call(
         product_kernel,
         out_shape=jax.ShapeDtypeStruct((256, 512), jnp.float32),
-        in_specs=[vmem, vmem, hbm, hbm],
+        in_specs=[vmem] * 4,
         out_specs=vmem,
         scratch_shapes=[
-            pltpu.VMEM(v.shape, v.dtype), pltpu.VMEM(w.shape, w.dtype),
             pltpu.VMEM((24, 256), jnp.int32), pltpu.SMEM((24, 256), jnp.int32),
-            dma, dma, dma,
+            pltpu.SemaphoreType.DMA,
         ],
         compiler_params=pltpu.CompilerParams(vmem_limit_bytes=40 * 2**20),
         name="product",

time: 152 us -> 145 us (0.954)
  Pallas kernels: 149 us -> 142 us
    pallas_call x1, Pallas kernels: 13.8 us -> 7.49 us  [product(): pl.pallas_call(product_kernel, out_shape=jax.ShapeDtypeStruct((256, 512),...]
    pallas_call x1, Pallas kernels: 20 us -> 18.2 us  [exchange(): pl.pallas_call(exchange_kernel, out_shape=jax.ShapeDtypeStruct((64, 8, 12...]
where the time goes in v3:
time: 145 us
  Pallas kernels  142 us (98%)
  local copies, waits for them, and re-layouts  2.49 us (2%)
    pallas_call x1, Pallas kernels, gather(): pl.pallas_call(gather_kernel, out_shape=(jax.ShapeDtypeStruct((NZ + 1, 8,...  116 us
    pallas_call x1, Pallas kernels, exchange(): pl.pallas_call(exchange_kernel, out_shape=jax.ShapeDtypeStruct((64, 8, 12...  18.2 us
    pallas_call x1, Pallas kernels, product(): pl.pallas_call(product_kernel, out_shape=jax.ShapeDtypeStruct((256, 512),...  7.49 us

profile of v3, /device:TPU:1, one launch (start us, length us, event | category | flops | bytes accessed | tf_op | source)
XLA Modules:
  0.0 145.2 jit_solution(2814551075868663704)
XLA Ops:
  0.0 0.7 pad_add_fusion
  0.7 0.0 copy-start
  0.7 0.9 copy-done
  1.6 0.0 copy-start.1
  1.6 0.9 copy-done.1
  2.5 116.3 %gather.1 = (bf16[33,8,3,2,16,128]{5,4,3,2,1,0:T(8,128)(2,1)S(1)}, s32[32,8,1,128]{3,2,1,0:T(1,128)S(1)}, bf16[65,3,4,16,128]{4,3,2,1,0:T(8,128)(2,1)S(1)}, s32[64,1,128]{2,1,0:T(1,128)S(1)}) custom-call(bf16[3,4,2,16,128]{4,3,2,1,0:T(8,128)(2,1)S(1)} %bitcast.15, bf16[3,4,2,16,128]{4,3,2,1,0:T(8,128)(2,1)S(1)} %bitcast.16, s32[2,1,128]{2,1,0:T(1,128)S(1)} %bitcast.18), custom_call_target="tpu_custom_call" | custom-call | tf_op jit(solution)/shard_map/gather/pallas_call | solution.py:187
  118.7 7.5 %product.1 = f32[256,512]{1,0:T(8,128)S(1)} custom-call(s32[256,128]{1,0:T(8,128)S(1)} %bitcast.14, s32[64,128]{1,0:T(8,128)S(1)} %bitcast.17, bf16[195,4,16,128]{3,2,1,0:T(8,128)(2,1)S(1)} %bitcast.11, bf16[792,2,16,128]{3,2,1,0:T(8,128)(2,1)S(1)} %bitcast.10), custom_call_target="tpu_custom_call" | custom-call | tf_op jit(solution)/shard_map/product/pallas_call | solution.py:264
  126.2 18.2 %exchange.1 = f32[64,8,128]{2,1,0:T(8,128)S(1)} custom-call(f32[4,4,2,8,512]{4,3,2,1,0:T(8,128)S(1)} %bitcast.12), custom_call_target="tpu_custom_call" | custom-call | tf_op jit(solution)/shard_map/exchange/pallas_call | solution.py:338
  144.5 0.7 copy.6
  (1 shorter events, 0.0 us)
Async XLA Ops:
  0.7 0.9 copy-start
  1.6 0.9 copy-start.1

commit v4 on v3

--- a/solution.py
+++ b/solution.py
@@ -204,9 +204,8 @@
     )(xb, qb, meta)
 
 
-def product_kernel(wm, vm, v, w, out, rows, tab, tab_sem):
+def tables_kernel(wm, vm, rows):
     x, y, zh, zl, core = where_am_i()
-
     v_cols, w_cols = vm[...], wm[...]
     first = v_cols[0:1, 0:1]
     row = lax.broadcasted_iota(jnp.int32, (64, 128), 0) // 16
@@ -241,41 +240,21 @@
             m = b * 4 + mid
             rows[m:m + 1] = jnp.where(core == 0, of_x, of_q).astype(jnp.int32) + none_w
     rows[16:20] = in_v.astype(jnp.int32) + none_v
-    tab_in = pltpu.make_async_copy(rows, tab, tab_sem)
-    tab_in.start()
-    out[...] = jnp.zeros_like(out)
-    tab_in.wait()
-
-    def step(g, carry):
-        vs, ws = [], []
-        for u in range(GROUP):
-            at = g * GROUP + u
-            vs.append(jnp.concatenate([v[tab[16 + c, at]].reshape(64, 128) for c in range(4)], axis=0))
-            ws.append(jnp.concatenate([w[tab[m, at]].reshape(32, 128) for m in range(16)], axis=0))
-        left = jnp.concatenate(vs, axis=1)
-        right = jnp.concatenate(ws, axis=1)
-        out[...] += lax.dot_general(left, right, (((1,), (1,)), ((), ())), preferred_element_type=jnp.float32)
-        return carry
-    lax.fori_loop(0, WIN // GROUP, step, 0)
-
-
-def product(wm, vm, v, w):
+    rows[20:24] = jnp.zeros((4, 256), jnp.int32)
+
+
+def tables(wm, vm):
     vmem = pl.BlockSpec(memory_space=pltpu.VMEM)
     return pl.pallas_call(
-        product_kernel,
-        out_shape=jax.ShapeDtypeStruct((256, 512), jnp.float32),
-        in_specs=[vmem] * 4,
+        tables_kernel,
+        out_shape=jax.ShapeDtypeStruct((24, 256), jnp.int32),
+        in_specs=[vmem] * 2,
         out_specs=vmem,
-        scratch_shapes=[
-            pltpu.VMEM((24, 256), jnp.int32), pltpu.SMEM((24, 256), jnp.int32),
-            pltpu.SemaphoreType.DMA,
-        ],
-        compiler_params=pltpu.CompilerParams(vmem_limit_bytes=40 * 2**20),
-        name="product",
-    )(wm, vm, v, w)
-
-
-def exchange_kernel(t, out, half, total, got, half_send, half_recv, send_sem, recv_sem):
+        name="tables",
+    )(wm, vm)
+
+
+def product_kernel(tab, v, w, out, t, half, total, got, half_send, half_recv, send_sem, recv_sem):
     x, y, zh, zl, core = where_am_i()
     z = zh * 16 + zl
     chip = x * 4 + y
@@ -288,66 +267,106 @@
     lax.fori_loop(1, 16, greet, 0)
     partner = device(x, y, z, 1 - core)
     pl.semaphore_signal(bar, inc=1, device_id=partner, device_id_type=MESH)
+
+    def multiply(n, first, last):
+        def step(g, carry):
+            vs, ws = [], []
+            for u in range(GROUP):
+                at = g * GROUP + u
+                vs.append(jnp.concatenate([v[tab[16 + c, at]].reshape(64, 128) for c in range(4)], axis=0))
+                ws.append(jnp.concatenate([w[tab[n * 8 + m, at]].reshape(32, 128) for m in range(8)], axis=0))
+            left = jnp.concatenate(vs, axis=1)
+            right = jnp.concatenate(ws, axis=1)
+            more = lax.dot_general(left, right, (((1,), (1,)), ((), ())), preferred_element_type=jnp.float32)
+            t[n] += more.reshape(4, 4, 2, 8, 256)
+            return carry
+        lax.fori_loop(first, last, step, 0)
+
+    def swap(n, c):
+        return pltpu.make_async_remote_copy(
+            t.at[n, c, :, 1 - core], half.at[n, c], half_send.at[n, c], half_recv.at[n, c],
+            device_id=partner, device_id_type=MESH)
+
+    def copy(n, c, px):
+        return pltpu.make_async_remote_copy(
+            total.at[n, c, px], got.at[n, chip], send_sem.at[n, c, px], recv_sem.at[n, chip],
+            device_id=device(px, c, z, core), device_id_type=MESH)
+
+    order = [(y + k) % 4 for k in (2, 1, 3, 0)]
+
+    def swap_all(n):
+        for c in order:
+            swap(n, c).start()
+
+    def send_all(n):
+        for k, c in enumerate(order):
+            swap(n, c).wait_recv()
+            total[n, c] = t[n, c, :, core] + half[n, c]
+            for k2 in (2, 1, 3):
+                copy(n, c, (x + k2) % 4).start()
+            if k < 3:
+                copy(n, c, x).start()
+            else:
+                pltpu.make_async_copy(total.at[n, c, x], got.at[n, chip], recv_sem.at[n, chip]).start()
+
+    lane = lax.broadcasted_iota(jnp.int32, (8, 128), 1) // 32
+
+    def put_together(n):
+        for xs in range(4):
+            for ys in range(4):
+                chip2 = xs * 4 + ys
+                pltpu.make_async_copy(got.at[n, chip2], got.at[n, chip2], recv_sem.at[n, chip2]).wait()
+            for b2 in range(2):
+                b = n * 2 + b2
+                part = [got[n, xs * 4 + ys, :, b2 * 128:(b2 + 1) * 128] for ys in range(4)]
+                for mid in range(4):
+                    acc = None
+                    for ys in range(4):
+                        turn = ((ys - mid) * 32) % 128
+                        piece = pltpu.roll(part[ys], turn, axis=1) if turn else part[ys]
+                        acc = piece if acc is None else jnp.where(lane == ys, piece, acc)
+                    out[16 * ((xs - b) % 4) + 4 * mid + b] = 0.5 * acc
+
+    steps = WIN // GROUP
+    t[...] = jnp.zeros_like(t)
+    multiply(0, 0, steps)
     pl.semaphore_wait(bar, 16)
-
-    swap = pltpu.make_async_remote_copy(
-        t.at[:, :, 1 - core], half, half_send, half_recv, device_id=partner, device_id_type=MESH)
-    swap.start()
-    swap.wait_recv()
-    total[...] = t[:, :, core] + half[...]
-
-    def copy(k):
-        chip2 = (chip + k) % 16
-        return pltpu.make_async_remote_copy(
-            total.at[chip2 % 4, chip2 // 4], got.at[chip], send_sem.at[k], recv_sem.at[chip],
-            device_id=device(chip2 // 4, chip2 % 4, z, core), device_id_type=MESH)
-
-    def start(k, carry):
-        copy(k).start()
-        return carry
-    lax.fori_loop(1, 16, start, 0)
-    own = pltpu.make_async_copy(total.at[y, x], got.at[chip], recv_sem.at[chip])
-    own.start()
-    own.wait()
-    swap.wait_send()
-
-    def finish(k, carry):
-        chip2 = (chip + k) % 16
-        pltpu.make_async_copy(got.at[chip2], got.at[chip2], recv_sem.at[chip2]).wait()
-        copy(k).wait_send()
-        return carry
-    lax.fori_loop(1, 16, finish, 0)
-
-    lane = lax.broadcasted_iota(jnp.int32, (8, 128), 1) // 32
-    for xs in range(4):
-        for b in range(4):
-            part = [got[xs * 4 + ys, :, b * 128:(b + 1) * 128] for ys in range(4)]
-            for mid in range(4):
-                acc = None
-                for ys in range(4):
-                    turn = ((ys - mid) * 32) % 128
-                    piece = pltpu.roll(part[ys], turn, axis=1) if turn else part[ys]
-                    acc = piece if acc is None else jnp.where(lane == ys, piece, acc)
-                out[16 * ((xs - b) % 4) + 4 * mid + b] = 0.5 * acc
-
-
-def exchange(t):
+    swap_all(0)
+    multiply(1, 0, 2)
+    send_all(0)
+    multiply(1, 2, steps)
+    swap_all(1)
+    send_all(1)
+    put_together(0)
+    put_together(1)
+    for n in range(2):
+        for k, c in enumerate(order):
+            swap(n, c).wait_send()
+            for k2 in (2, 1, 3):
+                copy(n, c, (x + k2) % 4).wait_send()
+            if k < 3:
+                copy(n, c, x).wait_send()
+
+
+def product(tab, v, w):
     dma = pltpu.SemaphoreType.DMA
     vmem = pl.BlockSpec(memory_space=pltpu.VMEM)
+    smem = pl.BlockSpec(memory_space=pltpu.SMEM)
     f32 = jnp.float32
     return pl.pallas_call(
-        exchange_kernel,
+        product_kernel,
         out_shape=jax.ShapeDtypeStruct((64, 8, 128), f32),
-        in_specs=[vmem],
+        in_specs=[smem, vmem, vmem],
         out_specs=vmem,
         scratch_shapes=[
-            pltpu.VMEM((4, 4, 8, 512), f32), pltpu.VMEM((4, 4, 8, 512), f32), pltpu.VMEM((16, 8, 512), f32),
-            dma, dma, dma((16,)), dma((16,)),
+            pltpu.VMEM((2, 4, 4, 2, 8, 256), f32), pltpu.VMEM((2, 4, 4, 8, 256), f32),
+            pltpu.VMEM((2, 4, 4, 8, 256), f32), pltpu.VMEM((2, 16, 8, 256), f32),
+            dma((2, 4)), dma((2, 4)), dma((2, 4, 4)), dma((2, 16)),
         ],
         compiler_params=pltpu.CompilerParams(
-            collective_id=1, has_side_effects=True, vmem_limit_bytes=16 * 2**20),
-        name="exchange",
-    )(t)
+            collective_id=1, has_side_effects=True, vmem_limit_bytes=40 * 2**20),
+        name="product",
+    )(tab, v, w)
 
 
 def shards(x_blocks, x_cols, q_blocks, q_cols):
@@ -355,10 +374,10 @@
     qb = q_blocks.reshape(3, 4, 2, 16, 128)
     meta = jnp.pad(jnp.stack([x_cols, q_cols[0]]), ((0, 0), (0, 125))).reshape(2, 1, 128)
     w, wm, v, vm = gather(xb, qb, meta)
-    t = product(
-        wm.reshape(NZ * 8, 128), vm.reshape(64, 128),
+    out = product(
+        tables(wm.reshape(NZ * 8, 128), vm.reshape(64, 128)),
         v.reshape(65 * 3, 4, 16, 128), w.reshape((NZ + 1) * 24, 2, 16, 128))
-    return exchange(t.reshape(4, 4, 2, 8, 512))[None]
+    return out[None]
 
 
 def solution(mesh):

time: 145 us -> 154 us (1.062)
  local copies, waits for them, and re-layouts: 2.49 us -> 10 us
    unnamed x5 -> x15, local copies, waits for them, and re-layouts: 2.48 us -> 10 us
where the time goes in v4:
time: 154 us; the launch traced here: 153 us
  Pallas kernels  143 us (93%)
  local copies, waits for them, and re-layouts  10 us (6%)
    pallas_call x1, Pallas kernels, gather(): pl.pallas_call(gather_kernel, out_shape=(jax.ShapeDtypeStruct((NZ + 1, 8,...  116 us
    pallas_call x1, Pallas kernels, product(): pl.pallas_call(product_kernel, out_shape=jax.ShapeDtypeStruct((64, 8, 128...  24.3 us
    unnamed x15, local copies, waits for them, and re-layouts  10 us

profile of v4, /device:TPU:1, one launch (start us, length us, event | category | flops | bytes accessed | tf_op | source)
XLA Modules:
  0.0 153.3 jit_solution(10876363968906429918)
XLA Ops:
  0.0 0.7 pad_add_fusion
  0.7 0.0 copy-start.3
  0.7 0.9 copy-done.3
  1.6 0.0 copy-start.4
  1.6 0.9 copy-done.4
  2.5 116.3 %gather.1 = (bf16[33,8,3,2,16,128]{5,4,3,2,1,0:T(8,128)(2,1)S(1)}, s32[32,8,1,128]{3,2,1,0:T(1,128)S(1)}, bf16[65,3,4,16,128]{4,3,2,1,0:T(8,128)(2,1)S(1)}, s32[64,1,128]{2,1,0:T(1,128)S(1)}) custom-call(bf16[3,4,2,16,128]{4,3,2,1,0:T(8,128)(2,1)S(1)} %bitcast.13, bf16[3,4,2,16,128]{4,3,2,1,0:T(8,128)(2,1)S(1)} %bitcast.14, s32[2,1,128]{2,1,0:T(1,128)S(1)} %bitcast.16), custom_call_target="tpu_custom_call" | custom-call | tf_op jit(solution)/shard_map/gather/pallas_call | solution.py:187
  118.7 0.0 copy-start
  118.8 2.7 %copy-done = bf16[33,8,3,2,16,128]{5,4,3,2,1,0:T(8,128)(2,1)} copy-done((bf16[33,8,3,2,16,128]{5,4,3,2,1,0:T(8,128)(2,1)}, bf16[33,8,3,2,16,128]{5,4,3,2,1,0:T(8,128)(2,1)S(1)}, u32[]{:S(2)}) %copy-start) | copy-done | bytes 6488088
  121.5 0.0 copy-start.2
  121.5 0.7 copy-done.2
  122.1 0.0 copy-start.6
  122.1 0.6 copy-done.6
  122.7 2.0 %tables.1.tab = s32[24,256]{1,0:T(8,128)} custom-call(s32[256,128]{1,0:T(8,128)} %bitcast.12, s32[64,128]{1,0:T(8,128)} %bitcast.15), custom_call_target="tpu_custom_call" | custom-call | tf_op jit(solution)/shard_map/tables/pallas_call | solution.py:248
  124.8 0.0 copy-start.1
  124.8 2.8 %copy-done.1 = bf16[33,8,3,2,16,128]{5,4,3,2,1,0:T(8,128)(2,1)S(1)} copy-done((bf16[33,8,3,2,16,128]{5,4,3,2,1,0:T(8,128)(2,1)S(1)}, bf16[33,8,3,2,16,128]{5,4,3,2,1,0:T(8,128)(2,1)}, u32[]{:S(2)}) %copy-start.1) | copy-done | bytes 6488088
  127.6 0.0 copy-start.5
  127.6 0.7 copy-done.5
  128.3 24.3 %product.1 = f32[64,8,128]{2,1,0:T(8,128)S(1)} custom-call(s32[24,256]{1,0:T(8,128)S(1)} %copy-done.5, bf16[195,4,16,128]{3,2,1,0:T(8,128)(2,1)S(1)} %bitcast.10, bf16[792,2,16,128]{3,2,1,0:T(8,128)(2,1)S(1)} %bitcast.9), custom_call_target="tpu_custom_call" | custom-call | tf_op jit(solution)/shard_map/product/pallas_call | solution.py:356
  152.6 0.7 copy.6
  (1 shorter events, 0.0 us)
Async XLA Ops:
  0.7 0.9 copy-start.3
  1.6 0.9 copy-start.4
  118.7 2.7 %copy-start = (bf16[33,8,3,2,16,128]{5,4,3,2,1,0:T(8,128)(2,1)}, bf16[33,8,3,2,16,128]{5,4,3,2,1,0:T(8,128)(2,1)S(1)}, u32[]{:S(2)}) copy-start(bf16[33,8,3,2,16,128]{5,4,3,2,1,0:T(8,128)(2,1)S(1)} %get-tuple-element.12) | copy-start | bytes 19464196
  121.5 0.7 copy-start.2
  122.1 0.6 copy-start.6
  124.8 2.8 %copy-start.1 = (bf16[33,8,3,2,16,128]{5,4,3,2,1,0:T(8,128)(2,1)S(1)}, bf16[33,8,3,2,16,128]{5,4,3,2,1,0:T(8,128)(2,1)}, u32[]{:S(2)}) copy-start(bf16[33,8,3,2,16,128]{5,4,3,2,1,0:T(8,128)(2,1)} %copy-done) | copy-start | bytes 19464196
  127.6 0.7 copy-start.5

commit v5 on v3

--- a/solution.py
+++ b/solution.py
@@ -22,6 +22,10 @@
 
 def device(x, y, z, core):
     return (x * 4 + (z // 16) * 2 + core, (z % 16) * 4 + y)
+
+
+def near(n):
+    return n + n // 2 * (5 - 2 * n)
 
 
 def gather_kernel(xb, qb, meta, w, wm, v, vm, w_send, w_recv, v_send, v_recv, ring_send, ring_recv):
@@ -97,15 +101,15 @@
         @pl.when((core == 0) & (half == (zl // 2) % 2) & (quarter == own))
         def _():
             def one(k, carry):
-                chip2 = (chip + k) % 16
-                to = device(chip2 // 4, chip2 % 4, z, 1)
+                px, py = (x + near(k // 4)) % 4, (y + near(k % 4)) % 4
+                to = device(px, py, z, 1)
                 g = quarter * 16 + place * 4
                 mine = pl.ds(zl % 2 * 4, 4)
                 pltpu.make_async_remote_copy(
                     w.at[plane, mine, :, zh], v.at[pl.ds(g, 4), :, y], v_send.at[0], v_recv.at[0],
                     device_id=to, device_id_type=MESH).start()
 
-                @pl.when(chip2 % 4 == y)
+                @pl.when(py == y)
                 def _():
                     pltpu.make_async_remote_copy(
                         wm.at[plane, mine], vm.at[pl.ds(g, 4)], v_send.at[1], v_recv.at[1],
@@ -116,14 +120,14 @@
         @pl.when((core == 1) & (plane % 16 == zl))
         def _():
             def one(k, carry):
-                chip2 = (chip + k) % 16
-                to = device(chip2 // 4, chip2 % 4, z, 0)
+                px, py = (x + near(k // 4)) % 4, (y + near(k % 4)) % 4
+                to = device(px, py, z, 0)
                 g = own * 16 + half * 8
                 pltpu.make_async_remote_copy(
                     w.at[plane, :, :, zh], v.at[pl.ds(g, 8), :, y], v_send.at[0], v_recv.at[0],
                     device_id=to, device_id_type=MESH).start()
 
-                @pl.when(chip2 % 4 == y)
+                @pl.when(py == y)
                 def _():
                     pltpu.make_async_remote_copy(
                         wm.at[plane], vm.at[pl.ds(g, 8)], v_send.at[1], v_recv.at[1],
@@ -290,36 +294,34 @@
     pl.semaphore_signal(bar, inc=1, device_id=partner, device_id_type=MESH)
     pl.semaphore_wait(bar, 16)
 
-    swap = pltpu.make_async_remote_copy(
-        t.at[:, :, 1 - core], half, half_send, half_recv, device_id=partner, device_id_type=MESH)
-    swap.start()
-    swap.wait_recv()
-    total[...] = t[:, :, core] + half[...]
-
-    def copy(k):
-        chip2 = (chip + k) % 16
+    def swap(c):
         return pltpu.make_async_remote_copy(
-            total.at[chip2 % 4, chip2 // 4], got.at[chip], send_sem.at[k], recv_sem.at[chip],
-            device_id=device(chip2 // 4, chip2 % 4, z, core), device_id_type=MESH)
-
-    def start(k, carry):
-        copy(k).start()
-        return carry
-    lax.fori_loop(1, 16, start, 0)
-    own = pltpu.make_async_copy(total.at[y, x], got.at[chip], recv_sem.at[chip])
-    own.start()
-    own.wait()
-    swap.wait_send()
-
-    def finish(k, carry):
-        chip2 = (chip + k) % 16
-        pltpu.make_async_copy(got.at[chip2], got.at[chip2], recv_sem.at[chip2]).wait()
-        copy(k).wait_send()
-        return carry
-    lax.fori_loop(1, 16, finish, 0)
+            t.at[c, :, 1 - core], half.at[c], half_send.at[c], half_recv.at[c],
+            device_id=partner, device_id_type=MESH)
+
+    def copy(c, px):
+        return pltpu.make_async_remote_copy(
+            total.at[c, px], got.at[chip], send_sem.at[c, px], recv_sem.at[chip],
+            device_id=device(px, c, z, core), device_id_type=MESH)
+
+    order = [(y + k) % 4 for k in (2, 1, 3, 0)]
+    for c in order:
+        swap(c).start()
+    for n, c in enumerate(order):
+        swap(c).wait_recv()
+        total[c] = t[c, :, core] + half[c]
+        for k in (2, 1, 3):
+            copy(c, (x + k) % 4).start()
+        if n < 3:
+            copy(c, x).start()
+        else:
+            pltpu.make_async_copy(total.at[c, x], got.at[chip], recv_sem.at[chip]).start()
 
     lane = lax.broadcasted_iota(jnp.int32, (8, 128), 1) // 32
     for xs in range(4):
+        for ys in range(4):
+            chip2 = xs * 4 + ys
+            pltpu.make_async_copy(got.at[chip2], got.at[chip2], recv_sem.at[chip2]).wait()
         for b in range(4):
             part = [got[xs * 4 + ys, :, b * 128:(b + 1) * 128] for ys in range(4)]
             for mid in range(4):
@@ -329,6 +331,12 @@
                     piece = pltpu.roll(part[ys], turn, axis=1) if turn else part[ys]
                     acc = piece if acc is None else jnp.where(lane == ys, piece, acc)
                 out[16 * ((xs - b) % 4) + 4 * mid + b] = 0.5 * acc
+    for n, c in enumerate(order):
+        swap(c).wait_send()
+        for k in (2, 1, 3):
+            copy(c, (x + k) % 4).wait_send()
+        if n < 3:
+            copy(c, x).wait_send()
 
 
 def exchange(t):
@@ -342,7 +350,7 @@
         out_specs=vmem,
         scratch_shapes=[
             pltpu.VMEM((4, 4, 8, 512), f32), pltpu.VMEM((4, 4, 8, 512), f32), pltpu.VMEM((16, 8, 512), f32),
-            dma, dma, dma((16,)), dma((16,)),
+            dma((4,)), dma((4,)), dma((4, 4)), dma((16,)),
         ],
         compiler_params=pltpu.CompilerParams(
             collective_id=1, has_side_effects=True, vmem_limit_bytes=16 * 2**20),

time: 145 us -> 143 us (0.986)
  Pallas kernels: 142 us -> 139 us
    pallas_call x1, Pallas kernels: 18.2 us -> 16.4 us  [exchange(): pl.pallas_call(exchange_kernel, out_shape=jax.ShapeDtypeStruct((64, 8, 12...]
where the time goes in v5:
time: 143 us; the launch traced here: 142 us
  Pallas kernels  139 us (97%)
  local copies, waits for them, and re-layouts  2.49 us (2%)
    pallas_call x1, Pallas kernels, gather(): pl.pallas_call(gather_kernel, out_shape=(jax.ShapeDtypeStruct((NZ + 1, 8,...  115 us
    pallas_call x1, Pallas kernels, exchange(): pl.pallas_call(exchange_kernel, out_shape=jax.ShapeDtypeStruct((64, 8, 12...  16.4 us
    pallas_call x1, Pallas kernels, product(): pl.pallas_call(product_kernel, out_shape=jax.ShapeDtypeStruct((256, 512),...  7.5 us

profile of v5, /device:TPU:1, one launch (start us, length us, event | category | flops | bytes accessed | tf_op | source)
XLA Modules:
  0.0 142.5 jit_solution(6260357479132906878)
XLA Ops:
  0.0 0.7 pad_add_fusion
  0.7 0.0 copy-start
  0.7 0.9 copy-done
  1.6 0.0 copy-start.1
  1.6 0.9 copy-done.1
  2.5 115.3 %gather.1 = (bf16[33,8,3,2,16,128]{5,4,3,2,1,0:T(8,128)(2,1)S(1)}, s32[32,8,1,128]{3,2,1,0:T(1,128)S(1)}, bf16[65,3,4,16,128]{4,3,2,1,0:T(8,128)(2,1)S(1)}, s32[64,1,128]{2,1,0:T(1,128)S(1)}) custom-call(bf16[3,4,2,16,128]{4,3,2,1,0:T(8,128)(2,1)S(1)} %bitcast.15, bf16[3,4,2,16,128]{4,3,2,1,0:T(8,128)(2,1)S(1)} %bitcast.16, s32[2,1,128]{2,1,0:T(1,128)S(1)} %bitcast.18), custom_call_target="tpu_custom_call" | custom-call | tf_op jit(solution)/shard_map/gather/pallas_call | solution.py:191
  117.8 7.5 %product.1 = f32[256,512]{1,0:T(8,128)S(1)} custom-call(s32[256,128]{1,0:T(8,128)S(1)} %bitcast.14, s32[64,128]{1,0:T(8,128)S(1)} %bitcast.17, bf16[195,4,16,128]{3,2,1,0:T(8,128)(2,1)S(1)} %bitcast.11, bf16[792,2,16,128]{3,2,1,0:T(8,128)(2,1)S(1)} %bitcast.10), custom_call_target="tpu_custom_call" | custom-call | tf_op jit(solution)/shard_map/product/pallas_call | solution.py:268
  125.3 16.4 %exchange.1 = f32[64,8,128]{2,1,0:T(8,128)S(1)} custom-call(f32[4,4,2,8,512]{4,3,2,1,0:T(8,128)S(1)} %bitcast.12), custom_call_target="tpu_custom_call" | custom-call | tf_op jit(solution)/shard_map/exchange/pallas_call | solution.py:346
  141.8 0.7 copy.6
  (1 shorter events, 0.0 us)
Async XLA Ops:
  0.7 0.9 copy-start
  1.6 0.9 copy-start.1
